TPU v7x, 32 devices: a whole 2x2x4 slice. The times are simulated.
32 devices in a mesh: box: 8 (over z, x), src: 4 (over y, core).
Axes of the slice: x: 2, y: 2, z: 4, core: 2. Of those that a mesh axis runs over, the one named last changes fastest.
Arguments:
- source_field: bfloat16 [512, 65536], P('src', 'box'), parts along dimension 0, may hold values from -6 to 6
- project_mats: bfloat16 [512, 128], P('box'), may hold values from -0.5 to 0.5
- local_mats: bfloat16 [8, 2, 512, 64], P(None, None, 'box'), may hold values from -0.75 to 0.75
- cross_mats: bfloat16 [6, 2, 512, 64], P(None, None, 'box'), may hold values from -0.75 to 0.75
- angles: bfloat16 [14, 65536], P(None, 'box'), may hold values from -3.140625 to 3.140625
- evaluate_mats: bfloat16 [1024, 64], P('box'), may hold values from -0.75 to 0.75
Outputs:
- image_blocks: bfloat16 [512, 65536], P('src', 'box'), parts along dimension 0
There are 4 independent parts, one for each index of `src`. A program takes and returns all parts, laid end to end along the dimension named above; an argument that names none is the same for every part. Nothing has to cross between parts.
All inputs are finite; a program needn't handle non-finite values.
Results may differ from a plain program's by a relative error of at most 0.024.
Values may be sent and summed in bfloat16 or wider, within the bound.
A program may use at most 128 MiB of HBM per device.

v0:
```python
import jax
import jax.numpy as jnp
from jax import lax
from jax.sharding import PartitionSpec as P


def swapped(x, axis, distance):
    return lax.ppermute(x, axis, [(i, i ^ 1 << distance) for i in range(lax.axis_size(axis))])


def flip_last(values, pair_span):
    full_shape = values.shape
    leading = full_shape[:-1]
    reshaped = values.reshape(leading + (full_shape[-1] // (2 * pair_span), 2, pair_span))
    return jnp.flip(reshaped, axis=-2).reshape(full_shape)


def mix_local(matrices, current, partner, phase_row):
    own_term = jnp.dot(matrices[0], current, preferred_element_type=jnp.float32)
    partner_term = jnp.dot(matrices[1], partner, preferred_element_type=jnp.float32)
    return (jnp.cos(phase_row)[None] * own_term + jnp.sin(phase_row)[None] * partner_term).astype(
        jnp.bfloat16
    )


def shards(source_field, project_mats, local_mats, cross_mats, angles, evaluate_mats):
    box_count = lax.axis_size("box")
    local_boxes = source_field.shape[1]
    rank_dim = project_mats.shape[0]
    pixel_rows = evaluate_mats.shape[0]
    local_levels = local_mats.shape[0]
    cross_levels = cross_mats.shape[0]
    group_size = local_boxes // box_count
    local_bits = (local_boxes & -local_boxes).bit_length() - 1
    box_bits = box_count.bit_length() - 1
    phases = angles.astype(jnp.float32)
    current = jnp.dot(project_mats, source_field, preferred_element_type=jnp.float32).astype(
        jnp.bfloat16
    )
    for level_idx in range(local_levels):
        partner = flip_last(current, 1 << level_idx % local_bits)
        current = mix_local(local_mats[level_idx], current, partner, phases[level_idx])
    for level_idx in range(cross_levels):
        level_bit = (box_bits - 1 - level_idx) % box_bits
        partner = swapped(current, "box", level_bit)
        current = mix_local(
            cross_mats[level_idx], current, partner, phases[local_levels + level_idx]
        )
    shaped = current.reshape(rank_dim, box_count, group_size)
    pixels_out = jnp.einsum(
        "qr,rdt->qdt",
        evaluate_mats,
        lax.all_to_all(shaped, "box", split_axis=1, concat_axis=1, tiled=True),
        preferred_element_type=jnp.float32,
    )
    return pixels_out.reshape(pixel_rows, local_boxes).astype(jnp.bfloat16)


def solution(mesh):
    in_specs = (
        P("src", "box"),
        P("box", None),
        P(None, None, "box", None),
        P(None, None, "box", None),
        P(None, "box"),
        P("box", None),
    )
    out_specs = P("src", "box")
    return jax.shard_map(shards, mesh=mesh, in_specs=in_specs, out_specs=out_specs, check_vma=False)
```

profile of v0, /device:TPU:0, one launch (start us, length us, event | category | flops | bytes accessed | tf_op | source)
XLA Modules:
  0.0 345.9 jit_solution(9864459853016983363)
XLA Ops:
  0.0 1.1 convert_element_type.99
  1.1 8.4 %slice_cosine_fusion.13 = (f32[1,8192]{1,0:T(1,128)}, f32[1,8192]{1,0:T(1,128)}, f32[1,8192]{1,0:T(1,128)}, f32[1,8192]{1,0:T(1,128)}, f32[1,8192]{1,0:T(1,128)}...) fusion(f32[14,8192]{1,0:T(8,128)S(1)} %convert_element_type.99), kind=kLoop, calls=%fused_computation.86 | loop fusion | bytes 589824 | tf_op jit(solution)/shard_map/cos | solution.py:21
  9.5 13.0 %slice_sine_fusion.13 = (f32[1,8192]{1,0:T(1,128)}, f32[1,8192]{1,0:T(1,128)}, f32[1,8192]{1,0:T(1,128)}, f32[1,8192]{1,0:T(1,128)}, f32[1,8192]{1,0:T(1,128)}, ...) fusion(f32[14,8192]{1,0:T(8,128)S(1)} %convert_element_type.99), kind=kLoop, calls=%fused_computation.85 | loop fusion | bytes 1081344 | tf_op jit(solution)/shard_map/sin | solution.py:21
  22.6 0.4 convolution_convert_fusion
  23.0 1.8 copy.9
  24.8 17.7 %rev.32 = bf16[64,4096,2,1]{0,2,1,3:T(2,128)(2,1)S(1)} reverse(bf16[64,4096,2,1]{0,2,1,3:T(2,128)(2,1)} %bitcast.193), dimensions={2} | reverse | bytes 2097152 | tf_op jit(solution)/shard_map/jit(_flip)/rev | solution.py:15
  42.5 1.6 convolution_multiply_fusion.27
  44.1 1.2 fusion.27
  45.2 1.8 copy.10
  47.0 3.2 rev.33
  50.3 1.6 convolution_multiply_fusion.26
  52.0 1.1 fusion.26
  53.1 1.8 copy.11
  54.9 2.4 rev.34
  57.3 0.8 convolution_multiply_fusion.25
  58.1 0.4 fusion.25
  58.6 1.8 copy.12
  60.4 2.0 rev.35
  62.3 0.8 convolution_multiply_fusion.24
  63.6 0.4 fusion.24
  64.0 1.8 copy.13
  65.7 2.0 rev.36
  67.7 0.9 convolution_multiply_fusion.23
  68.6 0.4 fusion.23
  69.0 1.8 copy.14
  70.8 2.0 rev.37
  72.9 0.8 convolution_multiply_fusion.22
  74.1 0.4 fusion.22
  74.5 3.3 reshape.121
  77.8 18.3 %rev.38 = bf16[64,64,2,64]{3,2,1,0:T(2,128)(2,1)S(1)} reverse(bf16[64,64,2,64]{3,2,1,0:T(2,128)(2,1)} %reshape.121), dimensions={2} | reverse | bytes 2097152 | tf_op jit(solution)/shard_map/jit(_flip)/rev | solution.py:15
  96.1 2.5 reshape.122
  98.6 1.6 convolution_multiply_fusion.14
  100.2 0.4 fusion.21
  100.7 0.8 reshape.123
  101.5 5.2 %rev.39 = bf16[64,32,2,128]{3,2,1,0:T(2,128)(2,1)S(1)} reverse(bf16[64,32,2,128]{3,2,1,0:T(2,128)(2,1)S(1)} %reshape.123), dimensions={2} | reverse | bytes 2097152 | tf_op jit(solution)/shard_map/jit(_flip)/rev | solution.py:15
  106.7 0.8 reshape.124
  108.3 0.4 fusion.20
  108.7 4.1 %collective-permute-start = (bf16[64,8192]{1,0:T(8,128)(2,1)S(1)}, bf16[64,8192]{1,0:T(8,128)(2,1)S(1)}, u32[]{:S(2)}, u32[]{:S(2)}) collective-permute-start(bf16[64,8192]{1,0:T(8,128)(2,1)S(1)} %bitcast.200), channel_id=1, source_target_pairs={{0,16},{4,20},{8,24},{12,28},{16,0},{20,4},{24,8},{28,12},{1,17},{... | collective-permute-start | bytes 3145736 | tf_op jit(solution)/shard_map/ppermute | solution.py:8
  112.8 1.1 convolution_multiply_fusion.11
  114.0 44.5 %collective-permute-done = bf16[64,8192]{1,0:T(8,128)(2,1)S(1)} collective-permute-done((bf16[64,8192]{1,0:T(8,128)(2,1)S(1)}, bf16[64,8192]{1,0:T(8,128)(2,1)S(1)}, u32[]{:S(2)}, u32[]{:S(2)}) %collective-permute-start) | collective-permute-done | bytes 1048608 | tf_op jit(solution)/shard_map/ppermute | solution.py:8
  158.4 1.1 fusion.19
  159.6 0.8 collective-permute-start.1
  160.4 1.1 convolution_multiply_fusion.9
  161.5 22.5 %collective-permute-done.1 = bf16[64,8192]{1,0:T(8,128)(2,1)S(1)} collective-permute-done((bf16[64,8192]{1,0:T(8,128)(2,1)S(1)}, bf16[64,8192]{1,0:T(8,128)(2,1)S(1)}, u32[]{:S(2)}, u32[]{:S(2)}) %collective-permute-start.1) | collective-permute-done | bytes 1048608 | tf_op jit(solution)/shard_map/ppermute | solution.py:8
  184.0 1.1 fusion.18
  185.2 1.3 collective-permute-start.2
  186.5 1.1 convolution_multiply_fusion.7
  187.6 21.0 %collective-permute-done.2 = bf16[64,8192]{1,0:T(8,128)(2,1)S(1)} collective-permute-done((bf16[64,8192]{1,0:T(8,128)(2,1)S(1)}, bf16[64,8192]{1,0:T(8,128)(2,1)S(1)}, u32[]{:S(2)}, u32[]{:S(2)}) %collective-permute-start.2) | collective-permute-done | bytes 1048608 | tf_op jit(solution)/shard_map/ppermute | solution.py:8
  208.7 1.1 fusion.17
  209.8 4.3 %collective-permute-start.3 = (bf16[64,8192]{1,0:T(8,128)(2,1)S(1)}, bf16[64,8192]{1,0:T(8,128)(2,1)S(1)}, u32[]{:S(2)}, u32[]{:S(2)}) collective-permute-start(bf16[64,8192]{1,0:T(8,128)(2,1)S(1)} %bitcast.203), channel_id=1, source_target_pairs={{0,16},{4,20},{8,24},{12,28},{16,0},{20,4},{24,8},{28,12},{1,17},{... | collective-permute-start | bytes 3145736 | tf_op jit(solution)/shard_map/ppermute | solution.py:8
  214.1 1.1 convolution_multiply_fusion.5
  215.3 43.2 %collective-permute-done.3 = bf16[64,8192]{1,0:T(8,128)(2,1)S(1)} collective-permute-done((bf16[64,8192]{1,0:T(8,128)(2,1)S(1)}, bf16[64,8192]{1,0:T(8,128)(2,1)S(1)}, u32[]{:S(2)}, u32[]{:S(2)}) %collective-permute-start.3) | collective-permute-done | bytes 1048608 | tf_op jit(solution)/shard_map/ppermute | solution.py:8
  258.5 1.1 fusion.16
  259.6 0.4 collective-permute-start.4
  260.1 1.1 convolution_multiply_fusion.3
  261.2 22.9 %collective-permute-done.4 = bf16[64,8192]{1,0:T(8,128)(2,1)S(1)} collective-permute-done((bf16[64,8192]{1,0:T(8,128)(2,1)S(1)}, bf16[64,8192]{1,0:T(8,128)(2,1)S(1)}, u32[]{:S(2)}, u32[]{:S(2)}) %collective-permute-start.4) | collective-permute-done | bytes 1048608 | tf_op jit(solution)/shard_map/ppermute | solution.py:8
  284.2 1.2 fusion.15
  285.3 1.6 collective-permute-start.5
  286.9 1.1 convolution_multiply_fusion.1
  288.0 20.9 %collective-permute-done.5 = bf16[64,8192]{1,0:T(8,128)(2,1)S(1)} collective-permute-done((bf16[64,8192]{1,0:T(8,128)(2,1)S(1)}, bf16[64,8192]{1,0:T(8,128)(2,1)S(1)}, u32[]{:S(2)}, u32[]{:S(2)}) %collective-permute-start.5) | collective-permute-done | bytes 1048608 | tf_op jit(solution)/shard_map/ppermute | solution.py:8
  308.9 1.1 fusion.14
  310.2 29.4 %all_to_all.5 = bf16[64,8,1024]{2,0,1:T(8,128)(2,1)S(1)} all-to-all(bf16[64,8,1024]{2,0,1:T(8,128)(2,1)S(1)} %bitcast.205), channel_id=1, replica_groups=mesh['box'=8,'src'=4] {'box'}, dimensions={1} | all-to-all | bytes 2097152 | tf_op jit(solution)/shard_map/all_to_all | solution.py:53
  339.5 2.1 convolution_convert_fusion.1
  341.7 4.2 %copy.16 = bf16[128,8192]{1,0:T(8,128)(2,1)} copy(bf16[128,8192]{0,1:T(8,128)(2,1)} %bitcast.192) | data formatting | bytes 4194304 | tf_op jit(solution)/shard_map/convert_element_type | solution.py:56
  (64 shorter events, 1.6 us)
Async XLA Ops:
  0.0 22.6 %copy-start = (bf16[128,8192]{1,0:T(8,128)(2,1)S(1)}, bf16[128,8192]{1,0:T(8,128)(2,1)}, u32[]{:S(2)}) copy-start(bf16[128,8192]{1,0:T(8,128)(2,1)} %param.6) | copy-start | bytes 6291460
  0.0 22.6 %copy-start.29 = (bf16[64,128]{1,0:T(8,128)(2,1)S(1)}, bf16[64,128]{1,0:T(8,128)(2,1)}, u32[]{:S(2)}) copy-start(bf16[64,128]{1,0:T(8,128)(2,1)} %param.7) | copy-start | bytes 49156
  45.2 1.8 copy-start.2
  50.3 1.7 copy-start.3
  54.9 2.4 copy-start.8
  57.2 0.9 copy-start.28
  58.6 1.8 copy-start.4
  62.3 1.2 copy-start.5
  62.3 1.2 copy-start.27
  67.7 0.9 copy-start.26
  69.0 1.8 copy-start.6
  72.9 1.2 copy-start.7
  72.9 1.2 copy-start.23
  96.1 2.5 copy-start.25
  98.6 1.7 copy-start.22
  101.5 6.1 %copy-start.24 = (f32[1,8192]{1,0:T(1,128)S(1)}, f32[1,8192]{1,0:T(1,128)}, u32[]{:S(2)}) copy-start(f32[1,8192]{1,0:T(1,128)} %get-tuple-element.11) | copy-start | bytes 98308
  107.5 0.8 copy-start.20
  108.3 4.6 %copy-start.18 = (f32[1,8192]{1,0:T(1,128)S(1)}, f32[1,8192]{1,0:T(1,128)}, u32[]{:S(2)}) copy-start(f32[1,8192]{1,0:T(1,128)} %get-tuple-element.28) | copy-start | bytes 98308
  108.7 49.7 %copy-start.21 = (f32[1,8192]{1,0:T(1,128)S(1)}, f32[1,8192]{1,0:T(1,128)}, u32[]{:S(2)}) copy-start(f32[1,8192]{1,0:T(1,128)} %get-tuple-element.10) | copy-start | bytes 98308
  108.7 49.7 %collective-permute-start = (bf16[64,8192]{1,0:T(8,128)(2,1)S(1)}, bf16[64,8192]{1,0:T(8,128)(2,1)S(1)}, u32[]{:S(2)}, u32[]{:S(2)}) collective-permute-start(bf16[64,8192]{1,0:T(8,128)(2,1)S(1)} %bitcast.200), channel_id=1, source_target_pairs={{0,16},{4,20},{8,24},{12,28},{16,0},{20,4},{24,8},{28,12},{1,17},{... | collective-permute-start | bytes 3145736 | tf_op jit(solution)/shard_map/ppermute | solution.py:8
  158.4 1.9 copy-start.16
  159.6 24.4 %copy-start.19 = (f32[1,8192]{1,0:T(1,128)S(1)}, f32[1,8192]{1,0:T(1,128)}, u32[]{:S(2)}) copy-start(f32[1,8192]{1,0:T(1,128)} %get-tuple-element.9) | copy-start | bytes 98308
  159.6 24.4 %collective-permute-start.1 = (bf16[64,8192]{1,0:T(8,128)(2,1)S(1)}, bf16[64,8192]{1,0:T(8,128)(2,1)S(1)}, u32[]{:S(2)}, u32[]{:S(2)}) collective-permute-start(bf16[64,8192]{1,0:T(8,128)(2,1)S(1)} %bitcast.201), channel_id=1, source_target_pairs={{0,8},{4,12},{8,0},{12,4},{16,24},{20,28},{24,16},{28,20},{1,9},{5... | collective-permute-start | bytes 3145736 | tf_op jit(solution)/shard_map/ppermute | solution.py:8
  184.0 2.5 copy-start.14
  185.2 23.5 %copy-start.17 = (f32[1,8192]{1,0:T(1,128)S(1)}, f32[1,8192]{1,0:T(1,128)}, u32[]{:S(2)}) copy-start(f32[1,8192]{1,0:T(1,128)} %get-tuple-element.8) | copy-start | bytes 98308
  185.2 23.5 %collective-permute-start.2 = (bf16[64,8192]{1,0:T(8,128)(2,1)S(1)}, bf16[64,8192]{1,0:T(8,128)(2,1)S(1)}, u32[]{:S(2)}, u32[]{:S(2)}) collective-permute-start(bf16[64,8192]{1,0:T(8,128)(2,1)S(1)} %bitcast.202), channel_id=1, source_target_pairs={{0,4},{4,0},{8,12},{12,8},{16,20},{20,16},{24,28},{28,24},{1,5},{5... | collective-permute-start | bytes 3145736 | tf_op jit(solution)/shard_map/ppermute | solution.py:8
  208.7 5.5 %copy-start.12 = (f32[1,8192]{1,0:T(1,128)S(1)}, f32[1,8192]{1,0:T(1,128)}, u32[]{:S(2)}) copy-start(f32[1,8192]{1,0:T(1,128)} %get-tuple-element.31) | copy-start | bytes 98308
  209.8 48.7 %copy-start.15 = (f32[1,8192]{1,0:T(1,128)S(1)}, f32[1,8192]{1,0:T(1,128)}, u32[]{:S(2)}) copy-start(f32[1,8192]{1,0:T(1,128)} %get-tuple-element.7) | copy-start | bytes 98308
  209.8 48.6 %collective-permute-start.3 = (bf16[64,8192]{1,0:T(8,128)(2,1)S(1)}, bf16[64,8192]{1,0:T(8,128)(2,1)S(1)}, u32[]{:S(2)}, u32[]{:S(2)}) collective-permute-start(bf16[64,8192]{1,0:T(8,128)(2,1)S(1)} %bitcast.203), channel_id=1, source_target_pairs={{0,16},{4,20},{8,24},{12,28},{16,0},{20,4},{24,8},{28,12},{1,17},{... | collective-permute-start | bytes 3145736 | tf_op jit(solution)/shard_map/ppermute | solution.py:8
  258.5 1.6 copy-start.10
  259.6 24.5 %copy-start.13 = (f32[1,8192]{1,0:T(1,128)S(1)}, f32[1,8192]{1,0:T(1,128)}, u32[]{:S(2)}) copy-start(f32[1,8192]{1,0:T(1,128)} %get-tuple-element.6) | copy-start | bytes 98308
  259.6 24.5 %collective-permute-start.4 = (bf16[64,8192]{1,0:T(8,128)(2,1)S(1)}, bf16[64,8192]{1,0:T(8,128)(2,1)S(1)}, u32[]{:S(2)}, u32[]{:S(2)}) collective-permute-start(bf16[64,8192]{1,0:T(8,128)(2,1)S(1)} %bitcast.204), channel_id=1, source_target_pairs={{0,8},{4,12},{8,0},{12,4},{16,24},{20,28},{24,16},{28,20},{1,9},{5... | collective-permute-start | bytes 3145736 | tf_op jit(solution)/shard_map/ppermute | solution.py:8
  284.2 2.7 copy-start.9
  285.3 23.6 %copy-start.11 = (f32[1,8192]{1,0:T(1,128)S(1)}, f32[1,8192]{1,0:T(1,128)}, u32[]{:S(2)}) copy-start(f32[1,8192]{1,0:T(1,128)} %get-tuple-element.5) | copy-start | bytes 98308
  285.3 23.6 %collective-permute-start.5 = (bf16[64,8192]{1,0:T(8,128)(2,1)S(1)}, bf16[64,8192]{1,0:T(8,128)(2,1)S(1)}, u32[]{:S(2)}, u32[]{:S(2)}) collective-permute-start(bf16[64,8192]{1,0:T(8,128)(2,1)S(1)} %bitcast.199), channel_id=1, source_target_pairs={{0,4},{4,0},{8,12},{12,8},{16,20},{20,16},{24,28},{28,24},{1,5},{5... | collective-permute-start | bytes 3145736 | tf_op jit(solution)/shard_map/ppermute | solution.py:8
  310.1 29.5 %copy-start.30 = (bf16[128,64]{0,1:T(8,128)(2,1)S(1)}, bf16[128,64]{0,1:T(8,128)(2,1)}, u32[]{:S(2)}) copy-start(bf16[128,64]{0,1:T(8,128)(2,1)} %param.11) | copy-start | bytes 49156
  341.7 4.2 %copy-start.1 = (bf16[128,8192]{1,0:T(8,128)(2,1)S(1)}, bf16[128,8192]{1,0:T(8,128)(2,1)}, u32[]{:S(2)}) copy-start(bf16[128,8192]{1,0:T(8,128)(2,1)} %param.6) | copy-start | bytes 6291460
where the time goes:
time: 349 us; the launch traced here: 346 us
  waiting for transfers between devices  175 us (50%)
  local copies, waits for them, and re-layouts  97.6 us (28%)
  matrix products  29.8 us (9%)
  blocking collectives  29.4 us (8%)
  starting transfers between devices  12.5 us (4%)
    ppermute x6, waiting for transfers between devices, swapped(): lax.ppermute(x, axis, [(i, i ^ 1 << distance) for i in range(lax.axis_siz...  175 us
    rev x8, local copies, waits for them, and re-layouts, flip_last(): return jnp.flip(reshaped, axis=-2).reshape(full_shape)  52.7 us
    all_to_all x1, blocking collectives, shards(): lax.all_to_all(shaped, 'box', split_axis=1, concat_axis=1, tiled=True)  29.4 us
    dot_general x14, matrix products, mix_local(): jnp.dot(matrices[1], partner, preferred_element_type=jnp.float32)  15.5 us
    sin x1, local copies, waits for them, and re-layouts, mix_local(): jnp.sin(phase_row)[None] * partner_term  13 us
    ppermute x6, starting transfers between devices, swapped(): lax.ppermute(x, axis, [(i, i ^ 1 << distance) for i in range(lax.axis_siz...  12.5 us
    dot_general x14, matrix products, mix_local(): own_term = jnp.dot(matrices[0], current, preferred_element_type=jnp.float32)  11.7 us
    convert_element_type x5, local copies, waits for them, and re-layouts, mix_local(): (jnp.cos(phase_row)[None] * own_term + jnp.sin(phase_row)[None] * partner...  8.91 us
  transfers between devices with their start and end apart: 6, of which 6 were waited for; matrix products, arithmetic and copies ran while one was open for 2% of the time, Pallas kernels for 0%

commit v1 on v0

--- a/solution.py
+++ b/solution.py
@@ -1,7 +1,18 @@
+import functools
+
 import jax
 import jax.numpy as jnp
 from jax import lax
+from jax.experimental import pallas as pl
+from jax.experimental.pallas import tpu as pltpu
 from jax.sharding import PartitionSpec as P
+
+MESH = pl.DeviceIdType.MESH
+F32 = jnp.float32
+BF16 = jnp.bfloat16
+LANES = 128
+TILE = 16
+UNIT = 256
 
 
 def swapped(x, axis, distance):
@@ -23,7 +34,7 @@
     )
 
 
-def shards(source_field, project_mats, local_mats, cross_mats, angles, evaluate_mats):
+def plain_shards(source_field, project_mats, local_mats, cross_mats, angles, evaluate_mats):
     box_count = lax.axis_size("box")
     local_boxes = source_field.shape[1]
     rank_dim = project_mats.shape[0]
@@ -56,6 +67,261 @@
     return pixels_out.reshape(pixel_rows, local_boxes).astype(jnp.bfloat16)
 
 
+def xor(a, b, bits):
+    out = 0
+    for i in range(bits):
+        out = out + lax.rem(a // (1 << i) + b // (1 << i), 2) * (1 << i)
+    return out
+
+
+def cos_sin(t):
+    u = t * 0.5
+    w = u * u
+    s = -1.0 / 39916800
+    for coef in (1.0 / 362880, -1.0 / 5040, 1.0 / 120, -1.0 / 6, 1.0):
+        s = s * w + coef
+    s = s * u
+    c = 1.0 / 479001600
+    for coef in (-1.0 / 3628800, 1.0 / 40320, -1.0 / 720, 1.0 / 24, -0.5, 1.0):
+        c = c * w + coef
+    return 1.0 - 2.0 * s * s, 2.0 * s * c
+
+
+def mix(matrix, own, partner, cos, sin):
+    stacked = jnp.concatenate([(cos * own).astype(BF16), (sin * partner).astype(BF16)], axis=0)
+    return jnp.dot(matrix, stacked, preferred_element_type=F32)
+
+
+def lane_partner(x, span):
+    lo, hi = x[:, :LANES], x[:, LANES:]
+    if span == LANES:
+        return jnp.concatenate([hi, lo], axis=1)
+    index = lax.broadcasted_iota(jnp.int32, lo.shape, 1)
+    index = jnp.bitwise_xor(index, span)
+    parts = [jnp.take_along_axis(p, index, axis=1, mode="promise_in_bounds") for p in (lo, hi)]
+    return jnp.concatenate(parts, axis=1)
+
+
+def kernel(
+    n_box, src_ref, proj_ref, local_ref, cross_ref, ang_ref, eval_ref, out_ref,
+    snd, rcv, aux, ang_out, phase, local_w, s_snd, s_rcv, w_snd, w_rcv, a_snd, a_rcv, q_snd, q_rcv,
+):
+    bits = n_box.bit_length() - 1
+    n_local, n_cross = local_ref.shape[0], cross_ref.shape[0]
+    rank = proj_ref.shape[0]
+    n_sub = rank // TILE
+    group = src_ref.shape[1] // n_box
+    w_rows = n_cross * TILE
+    me = lax.axis_index("box")
+    part = lax.axis_index("src")
+
+    def peer(d):
+        return xor(me, d, bits)
+
+    def to_box(d):
+        return (peer(d), part)
+
+    part_y, part_c = xor(part, 2, 2), xor(part, 1, 2)
+    barrier = pltpu.get_barrier_semaphore()
+    for target in [to_box(d) for d in range(1, n_box)] + [(me, part_y), (me, part_c)]:
+        pl.semaphore_signal(barrier, inc=1, device_id=target, device_id_type=MESH)
+
+    for m in range(n_cross):
+        rows = pl.ds(pl.multiple_of(part * TILE, TILE), TILE)
+        aux[part, me, m * TILE:(m + 1) * TILE, :] = jnp.concatenate(
+            [cross_ref[m, 0, rows, :], cross_ref[m, 1, rows, :]], axis=1
+        )
+    for l in range(n_local):
+        local_w[l] = jnp.concatenate([local_ref[l, 0], local_ref[l, 1]], axis=1)
+    phase[...] = jnp.zeros_like(phase)
+    phase[0:n_local + n_cross, :] = ang_ref[...].astype(F32)
+
+    def angle_tile(d):
+        start = pl.multiple_of(peer(d) * group + part * UNIT, UNIT)
+        block = phase[n_local:n_local + 8, pl.ds(start, UNIT)]
+        return jnp.concatenate([block[:, :LANES], block[:, LANES:]], axis=0).astype(BF16)
+
+    aux[part, me, w_rows:w_rows + TILE, :] = angle_tile(0)
+    for d in range(1, n_box):
+        ang_out[d] = angle_tile(d)
+
+    def w_copy(d):
+        low = d & -d
+        piece = aux.at[part, peer(d - low), 0:w_rows]
+        return pltpu.make_async_remote_copy(
+            src_ref=piece, dst_ref=piece, send_sem=w_snd.at[d], recv_sem=w_rcv.at[d],
+            device_id=to_box(low), device_id_type=MESH,
+        )
+
+    def a_copy(d):
+        return pltpu.make_async_remote_copy(
+            src_ref=ang_out.at[d], dst_ref=aux.at[part, me, w_rows:w_rows + TILE],
+            send_sem=a_snd.at[d], recv_sem=a_rcv.at[d],
+            device_id=to_box(d), device_id_type=MESH,
+        )
+
+    def q_copy(i):
+        quarter = part if i < 2 else part_y
+        return pltpu.make_async_remote_copy(
+            src_ref=aux.at[quarter], dst_ref=aux.at[quarter],
+            send_sem=q_snd.at[i], recv_sem=q_rcv.at[i],
+            device_id=(me, part_y if i == 0 else part_c), device_id_type=MESH,
+        )
+
+    def s_copy(sub, d):
+        return pltpu.make_async_remote_copy(
+            src_ref=snd.at[sub, d], dst_ref=rcv.at[sub, me],
+            send_sem=s_snd.at[sub, d], recv_sem=s_rcv.at[sub, d],
+            device_id=to_box(d), device_id_type=MESH,
+        )
+
+    waves = [[d for d in range(1, n_box) if d & -d == 1 << i] for i in range(bits - 1, -1, -1)]
+
+    pl.semaphore_wait(barrier, n_box + 1)
+    for d in waves[0]:
+        w_copy(d).start()
+    for d in range(n_box - 1, 0, -1):
+        a_copy(d).start()
+
+    half_boxes = n_box // 2
+
+    def local_step(it, carry):
+        sub, half = it // 2, lax.rem(it, 2)
+        first = half_boxes * (1 - half)
+        xs, cs, ss = [], [], []
+        for j in range(half_boxes):
+            start = pl.multiple_of(peer(first + j) * group + sub * UNIT, UNIT)
+            cols = pl.ds(start, UNIT)
+            xs.append(jnp.dot(proj_ref[...], src_ref[:, cols], preferred_element_type=F32))
+            cos, sin = cos_sin(phase[0:n_local, cols])
+            cs.append(cos)
+            ss.append(sin)
+        for l in range(n_local):
+            matrix = local_w[l]
+            for j in range(half_boxes):
+                x = xs[j]
+                xs[j] = mix(matrix, x, lane_partner(x, 1 << l), cs[j][l:l + 1], ss[j][l:l + 1])
+        for j in range(half_boxes):
+            snd[sub, first + j] = xs[j].astype(BF16)
+        for j in range(1, half_boxes):
+            s_copy(sub, first + j).start()
+
+        @pl.when(half == 0)
+        def _():
+            s_copy(sub, first).start()
+
+        @pl.when(half == 1)
+        def _():
+            rcv[sub, me] = xs[0].astype(BF16)
+
+        for i in range(1, bits):
+            @pl.when(it == i)
+            def _(i=i):
+                for d in waves[i - 1]:
+                    w_copy(d).wait_recv()
+                for d in waves[i]:
+                    w_copy(d).start()
+
+        @pl.when(it == bits + 1)
+        def _():
+            for d in waves[-1]:
+                w_copy(d).wait_recv()
+            for d in range(1, n_box):
+                a_copy(d).wait_recv()
+            q_copy(0).start()
+            q_copy(1).start()
+
+        @pl.when(it == bits + 3)
+        def _():
+            q_copy(0).wait_recv()
+            q_copy(2).start()
+
+        return carry
+
+    lax.fori_loop(0, 2 * n_sub, local_step, 0)
+    q_copy(1).wait_recv()
+    q_copy(2).wait_recv()
+
+    def cross_step(sub, carry):
+        for d in range(1, n_box):
+            s_copy(sub, d).wait_recv()
+        xs = [rcv[sub, k].astype(F32) for k in range(n_box)]
+        tables = [cos_sin(aux[sub, k, w_rows:w_rows + TILE, :].astype(F32)) for k in range(n_box)]
+
+        def row(table, m):
+            return jnp.concatenate([table[m:m + 1], table[8 + m:9 + m]], axis=1)
+
+        for m in range(n_cross):
+            bit = 1 << (bits - 1 - m) % bits
+            new = []
+            for k in range(n_box):
+                matrix = jnp.concatenate(
+                    [aux[q, k, m * TILE:(m + 1) * TILE, :] for q in range(n_sub)], axis=0
+                )
+                cos, sin = tables[k]
+                new.append(mix(matrix, xs[k], xs[k ^ bit], row(cos, m), row(sin, m)))
+            xs = new
+        for k in range(n_box):
+            pixels = jnp.dot(eval_ref[...], xs[k].astype(BF16), preferred_element_type=F32)
+            start = pl.multiple_of(k * group + sub * UNIT, UNIT)
+            out_ref[:, pl.ds(start, UNIT)] = pixels.astype(BF16)
+        return carry
+
+    lax.fori_loop(0, n_sub, cross_step, 0)
+
+    def drain(sub, carry):
+        for d in range(1, n_box):
+            s_copy(sub, d).wait_send()
+        return carry
+
+    lax.fori_loop(0, n_sub, drain, 0)
+    for d in range(1, n_box):
+        w_copy(d).wait_send()
+        a_copy(d).wait_send()
+    for i in range(3):
+        q_copy(i).wait_send()
+
+
+def shards(source_field, project_mats, local_mats, cross_mats, angles, evaluate_mats):
+    n_box = lax.axis_size("box")
+    rank = project_mats.shape[0]
+    n_sub = rank // TILE
+    n_cross = cross_mats.shape[0]
+    boxes = source_field.shape[1]
+    pixels = evaluate_mats.shape[0]
+    rows = n_cross * TILE + TILE
+    dma = pltpu.SemaphoreType.DMA
+    flops = 2 * boxes * rank * (2 * pixels + 2 * rank * angles.shape[0])
+    return pl.pallas_call(
+        functools.partial(kernel, n_box),
+        out_shape=jax.ShapeDtypeStruct((pixels, boxes), BF16),
+        in_specs=[pl.BlockSpec(memory_space=pltpu.VMEM)] * 6,
+        out_specs=pl.BlockSpec(memory_space=pltpu.VMEM),
+        scratch_shapes=[
+            pltpu.VMEM((n_sub, n_box, rank, UNIT), BF16),
+            pltpu.VMEM((n_sub, n_box, rank, UNIT), BF16),
+            pltpu.VMEM((n_sub, n_box, rows, LANES), BF16),
+            pltpu.VMEM((n_box, TILE, LANES), BF16),
+            pltpu.VMEM((2 * 8, boxes), F32),
+            pltpu.VMEM((local_mats.shape[0], rank, 2 * rank), BF16),
+            dma((n_sub, n_box)), dma((n_sub, n_box)),
+            dma((n_box,)), dma((n_box,)),
+            dma((n_box,)), dma((n_box,)),
+            dma((3,)), dma((3,)),
+        ],
+        compiler_params=pltpu.CompilerParams(
+            collective_id=0, has_side_effects=True, vmem_limit_bytes=48 * 1024 * 1024
+        ),
+        cost_estimate=pl.CostEstimate(
+            flops=flops, bytes_accessed=4 * boxes * pixels, transcendentals=0
+        ),
+    )(source_field, project_mats, local_mats, cross_mats, angles, evaluate_mats)
+
+
+def fits_kernel(mesh):
+    return mesh.shape["box"] == 8 and mesh.shape["src"] == 4
+
+
 def solution(mesh):
     in_specs = (
         P("src", "box"),
@@ -66,4 +332,5 @@
         P("box", None),
     )
     out_specs = P("src", "box")
-    return jax.shard_map(shards, mesh=mesh, in_specs=in_specs, out_specs=out_specs, check_vma=False)
+    body = shards if fits_kernel(mesh) else plain_shards
+    return jax.shard_map(body, mesh=mesh, in_specs=in_specs, out_specs=out_specs, check_vma=False)

time: 349 us -> 43.2 us (0.12)
  waiting for transfers between devices: 175 us -> 0 us
  local copies, waits for them, and re-layouts: 97.6 us -> 7.28 us
  Pallas kernels: 0 us -> 35.5 us
  matrix products: 29.8 us -> 0 us
  blocking collectives: 29.4 us -> 0 us
  starting transfers between devices: 12.5 us -> 0 us
    ppermute x6 -> x0, waiting for transfers between devices: 175 us -> none  [swapped(): lax.ppermute(x, axis, [(i, i ^ 1 << distance) for i in range(lax.axis_siz...]
    rev x8 -> x0, local copies, waits for them, and re-layouts: 52.7 us -> none  [flip_last(): return jnp.flip(reshaped, axis=-2).reshape(full_shape)]
    pallas_call x0 -> x1, Pallas kernels: none -> 35.5 us  [shards(): pl.pallas_call(functools.partial(kernel, n_box), out_shape=jax.ShapeDtype...]
    dot_general x30 -> x0, matrix products: 29.8 us -> none  [the longest x14 15.5 us: mix_local(): jnp.dot(matrices[1], partner, preferred_element_type=jnp.float32)]
    all_to_all x1 -> x0, blocking collectives: 29.4 us -> none  [shards(): lax.all_to_all(shaped, 'box', split_axis=1, concat_axis=1, tiled=True)]
    convert_element_type x7 -> x0, local copies, waits for them, and re-layouts: 14.9 us -> none  [the longest x5 8.91 us: mix_local(): (jnp.cos(phase_row)[None] * own_term + jnp.sin(phase_row)[None] * partner...]
    sin x1 -> x0, local copies, waits for them, and re-layouts: 13 us -> none  [mix_local(): jnp.sin(phase_row)[None] * partner_term]
    ppermute x6 -> x0, starting transfers between devices: 12.5 us -> none  [swapped(): lax.ppermute(x, axis, [(i, i ^ 1 << distance) for i in range(lax.axis_siz...]
  transfers between devices with their start and end apart: 6 -> 0, of which waited for: 6 -> 0; matrix products, arithmetic and copies ran while one was open for 2% -> 0% of each run, Pallas kernels for 0% -> 0%
where the time goes in v1:
time: 43.2 us; the launch traced here: 42.8 us
  Pallas kernels  35.5 us (82%)
  local copies, waits for them, and re-layouts  7.28 us (17%)
    pallas_call x1, Pallas kernels, shards(): pl.pallas_call(functools.partial(kernel, n_box), out_shape=jax.ShapeDtype...  35.5 us
    unnamed x12, local copies, waits for them, and re-layouts  7.28 us

profile of v1, /device:TPU:0, one launch (start us, length us, event | category | flops | bytes accessed | tf_op | source)
XLA Modules:
  0.0 42.8 jit_solution(17741600086155825150)
XLA Ops:
  0.0 0.8 %copy.7.eval_ref = bf16[128,64]{1,0:T(8,128)(2,1)S(1)} copy(bf16[128,64]{0,1:T(8,128)(2,1)} %param.11) | data formatting | bytes 32768 | tf_op args[5]
  0.8 0.0 copy-start
  0.8 1.6 %copy-done = bf16[128,8192]{1,0:T(8,128)(2,1)S(1)} copy-done((bf16[128,8192]{1,0:T(8,128)(2,1)S(1)}, bf16[128,8192]{1,0:T(8,128)(2,1)}, u32[]{:S(2)}) %copy-start) | copy-done | bytes 2097176
  2.4 0.0 copy-start.1
  2.4 0.9 %copy-done.1 = bf16[8,2,64,64]{3,2,1,0:T(8,128)(2,1)S(1)} copy-done((bf16[8,2,64,64]{3,2,1,0:T(8,128)(2,1)S(1)}, bf16[8,2,64,64]{3,2,1,0:T(8,128)(2,1)}, u32[]{:S(2)}) %copy-start.1) | copy-done | bytes 131096
  3.4 0.0 copy-start.2
  3.4 0.9 %copy-done.2 = bf16[14,8192]{1,0:T(8,128)(2,1)S(1)} copy-done((bf16[14,8192]{1,0:T(8,128)(2,1)S(1)}, bf16[14,8192]{1,0:T(8,128)(2,1)}, u32[]{:S(2)}) %copy-start.2) | copy-done | bytes 229400
  4.3 0.0 copy-start.3
  4.3 0.9 %copy-done.3 = bf16[6,2,64,64]{3,2,1,0:T(8,128)(2,1)S(1)} copy-done((bf16[6,2,64,64]{3,2,1,0:T(8,128)(2,1)S(1)}, bf16[6,2,64,64]{3,2,1,0:T(8,128)(2,1)}, u32[]{:S(2)}) %copy-start.3) | copy-done | bytes 98328
  5.3 0.0 copy-start.4
  5.3 0.7 %copy-done.4 = bf16[64,128]{1,0:T(8,128)(2,1)S(1)} copy-done((bf16[64,128]{1,0:T(8,128)(2,1)S(1)}, bf16[64,128]{1,0:T(8,128)(2,1)}, u32[]{:S(2)}) %copy-start.4) | copy-done | bytes 16408
  6.0 35.5 %shard_map.64 = bf16[128,8192]{1,0:T(8,128)(2,1)S(1)} custom-call(bf16[128,8192]{1,0:T(8,128)(2,1)S(1)} %copy-done, bf16[64,128]{1,0:T(8,128)(2,1)S(1)} %copy-done.4, bf16[8,2,64,64]{3,2,1,0:T(8,128)(2,1)S(1)} %copy-done.1, bf16[6,2,64,64]{3,2,1,0:T(8,128)(2,1)S(1)} %copy-done.3, bf16[14,8192]{1,0:T(8,128)(2,1)S(1)} %copy-done.2, ...), custom_call_target="tpu_custom_call" | custom-call | flops 2147483648 | bytes 4194304 | tf_op jit(solution)/shard_map/pallas_call | solution.py:295
  41.5 1.3 %copy.9 = bf16[128,8192]{1,0:T(8,128)(2,1)} copy(bf16[128,8192]{1,0:T(8,128)(2,1)S(1)} %shard_map.64) | data formatting | bytes 4194304
Async XLA Ops:
  0.8 1.6 %copy-start = (bf16[128,8192]{1,0:T(8,128)(2,1)S(1)}, bf16[128,8192]{1,0:T(8,128)(2,1)}, u32[]{:S(2)}) copy-start(bf16[128,8192]{1,0:T(8,128)(2,1)} %src_ref.1) | copy-start | bytes 6291460
  2.4 0.9 %copy-start.1 = (bf16[8,2,64,64]{3,2,1,0:T(8,128)(2,1)S(1)}, bf16[8,2,64,64]{3,2,1,0:T(8,128)(2,1)}, u32[]{:S(2)}) copy-start(bf16[8,2,64,64]{3,2,1,0:T(8,128)(2,1)} %local_ref.1) | copy-start | bytes 393220
  3.4 0.9 %copy-start.2 = (bf16[14,8192]{1,0:T(8,128)(2,1)S(1)}, bf16[14,8192]{1,0:T(8,128)(2,1)}, u32[]{:S(2)}) copy-start(bf16[14,8192]{1,0:T(8,128)(2,1)} %ang_ref.1) | copy-start | bytes 688132
  4.3 0.9 %copy-start.3 = (bf16[6,2,64,64]{3,2,1,0:T(8,128)(2,1)S(1)}, bf16[6,2,64,64]{3,2,1,0:T(8,128)(2,1)}, u32[]{:S(2)}) copy-start(bf16[6,2,64,64]{3,2,1,0:T(8,128)(2,1)} %cross_ref.1) | copy-start | bytes 294916
  5.3 0.7 %copy-start.4 = (bf16[64,128]{1,0:T(8,128)(2,1)S(1)}, bf16[64,128]{1,0:T(8,128)(2,1)}, u32[]{:S(2)}) copy-start(bf16[64,128]{1,0:T(8,128)(2,1)} %proj_ref.1) | copy-start | bytes 49156

commit v2 on v1

--- a/solution.py
+++ b/solution.py
@@ -103,14 +103,16 @@
 
 
 def kernel(
-    n_box, src_ref, proj_ref, local_ref, cross_ref, ang_ref, eval_ref, out_ref,
-    snd, rcv, aux, ang_out, phase, local_w, s_snd, s_rcv, w_snd, w_rcv, a_snd, a_rcv, q_snd, q_rcv,
+    n_box, src_hbm, proj_hbm, local_hbm, cross_hbm, ang_hbm, eval_hbm, out_hbm,
+    src_ref, proj_ref, local_ref, cross_ref, ang_ref, eval_t_ref, eval_ref,
+    snd, rcv, aux, ang_out, local_w, out_ref, in_sem, src_sem, out_sem,
+    s_snd, s_rcv, w_snd, w_rcv, a_snd, a_rcv, q_snd, q_rcv,
 ):
     bits = n_box.bit_length() - 1
     n_local, n_cross = local_ref.shape[0], cross_ref.shape[0]
     rank = proj_ref.shape[0]
     n_sub = rank // TILE
-    group = src_ref.shape[1] // n_box
+    group = src_hbm.shape[1] // n_box
     w_rows = n_cross * TILE
     me = lax.axis_index("box")
     part = lax.axis_index("src")
@@ -126,24 +128,63 @@
     for target in [to_box(d) for d in range(1, n_box)] + [(me, part_y), (me, part_c)]:
         pl.semaphore_signal(barrier, inc=1, device_id=target, device_id_type=MESH)
 
-    for m in range(n_cross):
-        rows = pl.ds(pl.multiple_of(part * TILE, TILE), TILE)
-        aux[part, me, m * TILE:(m + 1) * TILE, :] = jnp.concatenate(
-            [cross_ref[m, 0, rows, :], cross_ref[m, 1, rows, :]], axis=1
-        )
+    def load(i, source, target):
+        return pltpu.make_async_copy(source, target, in_sem.at[i])
+
+    loads = [
+        load(i, *pair)
+        for i, pair in enumerate([
+            (proj_hbm, proj_ref), (ang_hbm, ang_ref), (local_hbm, local_ref),
+            (cross_hbm, cross_ref), (eval_hbm, eval_t_ref),
+        ])
+    ]
+
+    def columns(sub, d):
+        return pl.ds(pl.multiple_of(peer(d) * group + sub * UNIT, UNIT), UNIT)
+
+    def load_source(sub, d):
+        return pltpu.make_async_copy(
+            src_hbm.at[:, columns(sub, d)], src_ref.at[sub, d], src_sem.at[sub, d]
+        )
+
+    def start_unit(it):
+        for j in range(half_boxes):
+            load_source(it // 2, half_boxes * (1 - lax.rem(it, 2)) + j).start()
+
+    half_boxes = n_box // 2
+    for copy in loads[:3]:
+        copy.start()
+    start_unit(0)
+    for copy in loads[3:]:
+        copy.start()
+
+    def start_rest(it, carry):
+        start_unit(it)
+        return carry
+
+    lax.fori_loop(1, 2 * n_sub, start_rest, 0)
+    for copy in loads[:3]:
+        copy.wait()
     for l in range(n_local):
         local_w[l] = jnp.concatenate([local_ref[l, 0], local_ref[l, 1]], axis=1)
-    phase[...] = jnp.zeros_like(phase)
-    phase[0:n_local + n_cross, :] = ang_ref[...].astype(F32)
 
     def angle_tile(d):
-        start = pl.multiple_of(peer(d) * group + part * UNIT, UNIT)
-        block = phase[n_local:n_local + 8, pl.ds(start, UNIT)]
+        block = ang_ref[:, columns(part, d)].astype(F32)[n_local:n_local + n_cross]
+        block = jnp.concatenate([block, jnp.zeros((8 - n_cross, UNIT), F32)], axis=0)
         return jnp.concatenate([block[:, :LANES], block[:, LANES:]], axis=0).astype(BF16)
 
-    aux[part, me, w_rows:w_rows + TILE, :] = angle_tile(0)
-    for d in range(1, n_box):
-        ang_out[d] = angle_tile(d)
+    def prepare_aux():
+        for copy in loads[3:]:
+            copy.wait()
+        for m in range(n_cross):
+            rows = pl.ds(pl.multiple_of(part * TILE, TILE), TILE)
+            aux[part, me, m * TILE:(m + 1) * TILE, :] = jnp.concatenate(
+                [cross_ref[m, 0, rows, :], cross_ref[m, 1, rows, :]], axis=1
+            )
+        aux[part, me, w_rows:w_rows + TILE, :] = angle_tile(0)
+        for d in range(1, n_box):
+            ang_out[d] = angle_tile(d)
+        eval_ref[...] = eval_t_ref[...].astype(F32).T.astype(BF16)
 
     def w_copy(d):
         low = d & -d
@@ -177,23 +218,16 @@
 
     waves = [[d for d in range(1, n_box) if d & -d == 1 << i] for i in range(bits - 1, -1, -1)]
 
-    pl.semaphore_wait(barrier, n_box + 1)
-    for d in waves[0]:
-        w_copy(d).start()
-    for d in range(n_box - 1, 0, -1):
-        a_copy(d).start()
-
-    half_boxes = n_box // 2
-
     def local_step(it, carry):
         sub, half = it // 2, lax.rem(it, 2)
         first = half_boxes * (1 - half)
         xs, cs, ss = [], [], []
         for j in range(half_boxes):
-            start = pl.multiple_of(peer(first + j) * group + sub * UNIT, UNIT)
-            cols = pl.ds(start, UNIT)
-            xs.append(jnp.dot(proj_ref[...], src_ref[:, cols], preferred_element_type=F32))
-            cos, sin = cos_sin(phase[0:n_local, cols])
+            load_source(sub, first + j).wait()
+            xs.append(
+                jnp.dot(proj_ref[...], src_ref[sub, first + j], preferred_element_type=F32)
+            )
+            cos, sin = cos_sin(ang_ref[:, columns(sub, first + j)].astype(F32)[:n_local])
             cs.append(cos)
             ss.append(sin)
         for l in range(n_local):
@@ -203,6 +237,11 @@
                 xs[j] = mix(matrix, x, lane_partner(x, 1 << l), cs[j][l:l + 1], ss[j][l:l + 1])
         for j in range(half_boxes):
             snd[sub, first + j] = xs[j].astype(BF16)
+
+        @pl.when(it == 0)
+        def _():
+            pl.semaphore_wait(barrier, n_box + 1)
+
         for j in range(1, half_boxes):
             s_copy(sub, first + j).start()
 
@@ -213,6 +252,14 @@
         @pl.when(half == 1)
         def _():
             rcv[sub, me] = xs[0].astype(BF16)
+
+        @pl.when(it == 0)
+        def _():
+            prepare_aux()
+            for d in waves[0]:
+                w_copy(d).start()
+            for d in range(n_box - 1, 0, -1):
+                a_copy(d).start()
 
         for i in range(1, bits):
             @pl.when(it == i)
@@ -241,6 +288,12 @@
     lax.fori_loop(0, 2 * n_sub, local_step, 0)
     q_copy(1).wait_recv()
     q_copy(2).wait_recv()
+
+    def store(sub, k):
+        start = pl.multiple_of(k * group + sub * UNIT, UNIT)
+        return pltpu.make_async_copy(
+            out_ref.at[sub, k], out_hbm.at[:, pl.ds(start, UNIT)], out_sem.at[sub, k]
+        )
 
     def cross_step(sub, carry):
         for d in range(1, n_box):
@@ -263,8 +316,8 @@
             xs = new
         for k in range(n_box):
             pixels = jnp.dot(eval_ref[...], xs[k].astype(BF16), preferred_element_type=F32)
-            start = pl.multiple_of(k * group + sub * UNIT, UNIT)
-            out_ref[:, pl.ds(start, UNIT)] = pixels.astype(BF16)
+            out_ref[sub, k] = pixels.astype(BF16)
+            store(sub, k).start()
         return carry
 
     lax.fori_loop(0, n_sub, cross_step, 0)
@@ -272,6 +325,8 @@
     def drain(sub, carry):
         for d in range(1, n_box):
             s_copy(sub, d).wait_send()
+        for k in range(n_box):
+            store(sub, k).wait()
         return carry
 
     lax.fori_loop(0, n_sub, drain, 0)
@@ -295,27 +350,35 @@
     return pl.pallas_call(
         functools.partial(kernel, n_box),
         out_shape=jax.ShapeDtypeStruct((pixels, boxes), BF16),
-        in_specs=[pl.BlockSpec(memory_space=pltpu.VMEM)] * 6,
-        out_specs=pl.BlockSpec(memory_space=pltpu.VMEM),
+        in_specs=[pl.BlockSpec(memory_space=pltpu.HBM)] * 6,
+        out_specs=pl.BlockSpec(memory_space=pltpu.HBM),
         scratch_shapes=[
+            pltpu.VMEM((n_sub, n_box, pixels, UNIT), BF16),
+            pltpu.VMEM(project_mats.shape, BF16),
+            pltpu.VMEM(local_mats.shape, BF16),
+            pltpu.VMEM(cross_mats.shape, BF16),
+            pltpu.VMEM(angles.shape, BF16),
+            pltpu.VMEM((rank, pixels), BF16),
+            pltpu.VMEM((pixels, rank), BF16),
             pltpu.VMEM((n_sub, n_box, rank, UNIT), BF16),
             pltpu.VMEM((n_sub, n_box, rank, UNIT), BF16),
             pltpu.VMEM((n_sub, n_box, rows, LANES), BF16),
             pltpu.VMEM((n_box, TILE, LANES), BF16),
-            pltpu.VMEM((2 * 8, boxes), F32),
             pltpu.VMEM((local_mats.shape[0], rank, 2 * rank), BF16),
+            pltpu.VMEM((n_sub, n_box, pixels, UNIT), BF16),
+            dma((5,)), dma((n_sub, n_box)), dma((n_sub, n_box)),
             dma((n_sub, n_box)), dma((n_sub, n_box)),
             dma((n_box,)), dma((n_box,)),
             dma((n_box,)), dma((n_box,)),
             dma((3,)), dma((3,)),
         ],
         compiler_params=pltpu.CompilerParams(
-            collective_id=0, has_side_effects=True, vmem_limit_bytes=48 * 1024 * 1024
+            collective_id=0, has_side_effects=True, vmem_limit_bytes=60 * 1024 * 1024
         ),
         cost_estimate=pl.CostEstimate(
             flops=flops, bytes_accessed=4 * boxes * pixels, transcendentals=0
         ),
-    )(source_field, project_mats, local_mats, cross_mats, angles, evaluate_mats)
+    )(source_field, project_mats, local_mats, cross_mats, angles, evaluate_mats.T)
 
 
 def fits_kernel(mesh):

time: 43.2 us -> 43.6 us (level)
  Pallas kernels: 35.5 us -> 40.2 us
  local copies, waits for them, and re-layouts: 7.28 us -> 3.1 us
    pallas_call x1, Pallas kernels: 35.5 us -> 40.2 us  [shards(): pl.pallas_call(functools.partial(kernel, n_box), out_shape=jax.ShapeDtype...]
    unnamed x12 -> x1, local copies, waits for them, and re-layouts: 7.28 us -> 3.1 us
where the time goes in v2:
time: 43.6 us; the launch traced here: 43.3 us
  Pallas kernels  40.2 us (92%)
  local copies, waits for them, and re-layouts  3.1 us (7%)
    pallas_call x1, Pallas kernels, shards(): pl.pallas_call(functools.partial(kernel, n_box), out_shape=jax.ShapeDtype...  40.2 us
    unnamed x1, local copies, waits for them, and re-layouts  3.1 us

profile of v2, /device:TPU:0, one launch (start us, length us, event | category | flops | bytes accessed | tf_op | source)
XLA Modules:
  0.0 43.3 jit_solution(8064062318418631773)
XLA Ops:
  0.0 40.2 %shard_map.64 = bf16[128,8192]{1,0:T(8,128)(2,1)} custom-call(bf16[128,8192]{1,0:T(8,128)(2,1)} %src_hbm.1, bf16[64,128]{1,0:T(8,128)(2,1)} %proj_hbm.1, bf16[8,2,64,64]{3,2,1,0:T(8,128)(2,1)} %local_hbm.1, bf16[6,2,64,64]{3,2,1,0:T(8,128)(2,1)} %cross_hbm.1, bf16[14,8192]{1,0:T(8,128)(2,1)} %ang_hbm.1, bf16[64,128]{1,0:T(8,128)(2,1)} %bitcast.1), custom_call_target="tpu_custom_call" | custom-call | flops 2147483648 | bytes 4194304 | tf_op jit(solution)/shard_map/pallas_call | solution.py:350
  40.2 3.1 %copy.8 = bf16[128,8192]{1,0:T(8,128)(2,1)} copy(bf16[128,8192]{1,0:T(8,128)(2,1)} %shard_map.64) | data formatting | bytes 4194304

commit v3 on v2

--- a/solution.py
+++ b/solution.py
@@ -103,9 +103,9 @@
 
 
 def kernel(
-    n_box, src_hbm, proj_hbm, local_hbm, cross_hbm, ang_hbm, eval_hbm, out_hbm,
+    n_box, src_hbm, proj_hbm, local_hbm, cross_hbm, ang_hbm, eval_hbm, out_ref,
     src_ref, proj_ref, local_ref, cross_ref, ang_ref, eval_t_ref, eval_ref,
-    snd, rcv, aux, ang_out, local_w, out_ref, in_sem, src_sem, out_sem,
+    snd, rcv, aux, ang_out, local_w, in_sem, src_sem,
     s_snd, s_rcv, w_snd, w_rcv, a_snd, a_rcv, q_snd, q_rcv,
 ):
     bits = n_box.bit_length() - 1
@@ -147,11 +147,13 @@
             src_hbm.at[:, columns(sub, d)], src_ref.at[sub, d], src_sem.at[sub, d]
         )
 
-    def start_unit(it):
-        for j in range(half_boxes):
-            load_source(it // 2, half_boxes * (1 - lax.rem(it, 2)) + j).start()
-
-    half_boxes = n_box // 2
+    far = n_box // 2
+    order = list(range(far, n_box)) + list(range(far - 1, -1, -1))
+
+    def start_unit(sub):
+        for d in order:
+            load_source(sub, d).start()
+
     for copy in loads[:3]:
         copy.start()
     start_unit(0)
@@ -162,7 +164,7 @@
         start_unit(it)
         return carry
 
-    lax.fori_loop(1, 2 * n_sub, start_rest, 0)
+    lax.fori_loop(1, n_sub, start_rest, 0)
     for copy in loads[:3]:
         copy.wait()
     for l in range(n_local):
@@ -187,7 +189,7 @@
         eval_ref[...] = eval_t_ref[...].astype(F32).T.astype(BF16)
 
     def w_copy(d):
-        low = d & -d
+        low = d if d <= far else d - far
         piece = aux.at[part, peer(d - low), 0:w_rows]
         return pltpu.make_async_remote_copy(
             src_ref=piece, dst_ref=piece, send_sem=w_snd.at[d], recv_sem=w_rcv.at[d],
@@ -216,84 +218,65 @@
             device_id=to_box(d), device_id_type=MESH,
         )
 
-    waves = [[d for d in range(1, n_box) if d & -d == 1 << i] for i in range(bits - 1, -1, -1)]
-
-    def local_step(it, carry):
-        sub, half = it // 2, lax.rem(it, 2)
-        first = half_boxes * (1 - half)
-        xs, cs, ss = [], [], []
-        for j in range(half_boxes):
-            load_source(sub, first + j).wait()
-            xs.append(
-                jnp.dot(proj_ref[...], src_ref[sub, first + j], preferred_element_type=F32)
-            )
-            cos, sin = cos_sin(ang_ref[:, columns(sub, first + j)].astype(F32)[:n_local])
-            cs.append(cos)
-            ss.append(sin)
+    def local_step(sub, carry):
+        xs, cs, ss = {}, {}, {}
+        for d in order:
+            load_source(sub, d).wait()
+        for d in order:
+            xs[d] = jnp.dot(proj_ref[...], src_ref[sub, d], preferred_element_type=F32)
+            cs[d], ss[d] = cos_sin(ang_ref[:, columns(sub, d)].astype(F32)[:n_local])
         for l in range(n_local):
+            if l == n_local // 2:
+                @pl.when(sub == 0)
+                def _():
+                    pl.semaphore_wait(barrier, n_box + 1)
+
+                @pl.when(sub == 1)
+                def _():
+                    w_copy(far).wait_recv()
+                    for d in range(far + 1, n_box):
+                        w_copy(d).start()
+
+                @pl.when(sub == n_sub - 1)
+                def _():
+                    q_copy(0).wait_recv()
+                    q_copy(2).start()
+
             matrix = local_w[l]
-            for j in range(half_boxes):
-                x = xs[j]
-                xs[j] = mix(matrix, x, lane_partner(x, 1 << l), cs[j][l:l + 1], ss[j][l:l + 1])
-        for j in range(half_boxes):
-            snd[sub, first + j] = xs[j].astype(BF16)
-
-        @pl.when(it == 0)
-        def _():
-            pl.semaphore_wait(barrier, n_box + 1)
-
-        for j in range(1, half_boxes):
-            s_copy(sub, first + j).start()
-
-        @pl.when(half == 0)
-        def _():
-            s_copy(sub, first).start()
-
-        @pl.when(half == 1)
-        def _():
-            rcv[sub, me] = xs[0].astype(BF16)
-
-        @pl.when(it == 0)
+            for d in order:
+                x = xs[d]
+                xs[d] = mix(matrix, x, lane_partner(x, 1 << l), cs[d][l:l + 1], ss[d][l:l + 1])
+        for d in order:
+            snd[sub, d] = xs[d].astype(BF16)
+
+        for d in order:
+            if d:
+                s_copy(sub, d).start()
+            else:
+                rcv[sub, me] = xs[0].astype(BF16)
+
+        @pl.when(sub == 0)
         def _():
             prepare_aux()
-            for d in waves[0]:
+            for d in range(far, 0, -1):
                 w_copy(d).start()
             for d in range(n_box - 1, 0, -1):
                 a_copy(d).start()
 
-        for i in range(1, bits):
-            @pl.when(it == i)
-            def _(i=i):
-                for d in waves[i - 1]:
+        @pl.when(sub == 1)
+        def _():
+            for d in range(1, n_box):
+                if d != far:
                     w_copy(d).wait_recv()
-                for d in waves[i]:
-                    w_copy(d).start()
-
-        @pl.when(it == bits + 1)
-        def _():
-            for d in waves[-1]:
-                w_copy(d).wait_recv()
-            for d in range(1, n_box):
                 a_copy(d).wait_recv()
             q_copy(0).start()
             q_copy(1).start()
 
-        @pl.when(it == bits + 3)
-        def _():
-            q_copy(0).wait_recv()
-            q_copy(2).start()
-
         return carry
 
-    lax.fori_loop(0, 2 * n_sub, local_step, 0)
+    lax.fori_loop(0, n_sub, local_step, 0)
     q_copy(1).wait_recv()
     q_copy(2).wait_recv()
-
-    def store(sub, k):
-        start = pl.multiple_of(k * group + sub * UNIT, UNIT)
-        return pltpu.make_async_copy(
-            out_ref.at[sub, k], out_hbm.at[:, pl.ds(start, UNIT)], out_sem.at[sub, k]
-        )
 
     def cross_step(sub, carry):
         for d in range(1, n_box):
@@ -316,8 +299,8 @@
             xs = new
         for k in range(n_box):
             pixels = jnp.dot(eval_ref[...], xs[k].astype(BF16), preferred_element_type=F32)
-            out_ref[sub, k] = pixels.astype(BF16)
-            store(sub, k).start()
+            start = pl.multiple_of(k * group + sub * UNIT, UNIT)
+            out_ref[:, pl.ds(start, UNIT)] = pixels.astype(BF16)
         return carry
 
     lax.fori_loop(0, n_sub, cross_step, 0)
@@ -325,8 +308,6 @@
     def drain(sub, carry):
         for d in range(1, n_box):
             s_copy(sub, d).wait_send()
-        for k in range(n_box):
-            store(sub, k).wait()
         return carry
 
     lax.fori_loop(0, n_sub, drain, 0)
@@ -349,9 +330,9 @@
     flops = 2 * boxes * rank * (2 * pixels + 2 * rank * angles.shape[0])
     return pl.pallas_call(
         functools.partial(kernel, n_box),
-        out_shape=jax.ShapeDtypeStruct((pixels, boxes), BF16),
+        out_shape=pltpu.VMEM((pixels, boxes), BF16),
         in_specs=[pl.BlockSpec(memory_space=pltpu.HBM)] * 6,
-        out_specs=pl.BlockSpec(memory_space=pltpu.HBM),
+        out_specs=pl.BlockSpec(memory_space=pltpu.VMEM),
         scratch_shapes=[
             pltpu.VMEM((n_sub, n_box, pixels, UNIT), BF16),
             pltpu.VMEM(project_mats.shape, BF16),
@@ -365,8 +346,7 @@
             pltpu.VMEM((n_sub, n_box, rows, LANES), BF16),
             pltpu.VMEM((n_box, TILE, LANES), BF16),
             pltpu.VMEM((local_mats.shape[0], rank, 2 * rank), BF16),
-            pltpu.VMEM((n_sub, n_box, pixels, UNIT), BF16),
-            dma((5,)), dma((n_sub, n_box)), dma((n_sub, n_box)),
+            dma((5,)), dma((n_sub, n_box)),
             dma((n_sub, n_box)), dma((n_sub, n_box)),
             dma((n_box,)), dma((n_box,)),
             dma((n_box,)), dma((n_box,)),

time: 43.6 us -> 37.6 us (0.86)
  Pallas kernels: 40.2 us -> 36.2 us
  local copies, waits for them, and re-layouts: 3.1 us -> 1.32 us
    pallas_call x1, Pallas kernels: 40.2 us -> 36.2 us  [shards(): pl.pallas_call(functools.partial(kernel, n_box), out_shape=pltpu.VMEM((pi...]
    unnamed x1, local copies, waits for them, and re-layouts: 3.1 us -> 1.32 us
where the time goes in v3:
time: 37.6 us; the launch traced here: 37.5 us
  Pallas kernels  36.2 us (96%)
  local copies, waits for them, and re-layouts  1.32 us (4%)
    pallas_call x1, Pallas kernels, shards(): pl.pallas_call(functools.partial(kernel, n_box), out_shape=pltpu.VMEM((pi...  36.2 us
    unnamed x1, local copies, waits for them, and re-layouts  1.32 us

profile of v3, /device:TPU:0, one launch (start us, length us, event | category | flops | bytes accessed | tf_op | source)
XLA Modules:
  0.0 37.5 jit_solution(3798745413267520323)
XLA Ops:
  0.0 36.2 %shard_map.64 = bf16[128,8192]{1,0:T(8,128)(2,1)S(1)} custom-call(bf16[128,8192]{1,0:T(8,128)(2,1)} %src_hbm.1, bf16[64,128]{1,0:T(8,128)(2,1)} %proj_hbm.1, bf16[8,2,64,64]{3,2,1,0:T(8,128)(2,1)} %local_hbm.1, bf16[6,2,64,64]{3,2,1,0:T(8,128)(2,1)} %cross_hbm.1, bf16[14,8192]{1,0:T(8,128)(2,1)} %ang_hbm.1, bf16[64,128]{1,0:T(8,128)(2,1)} %bitcast.1), custom_call_target="tpu_custom_call" | custom-call | flops 2147483648 | bytes 4194304 | tf_op jit(solution)/shard_map/pallas_call | solution.py:331
  36.2 1.3 %copy.8 = bf16[128,8192]{1,0:T(8,128)(2,1)} copy(bf16[128,8192]{1,0:T(8,128)(2,1)S(1)} %shard_map.64) | data formatting | bytes 4194304

commit v4 on v3

--- a/solution.py
+++ b/solution.py
@@ -186,7 +186,6 @@
         aux[part, me, w_rows:w_rows + TILE, :] = angle_tile(0)
         for d in range(1, n_box):
             ang_out[d] = angle_tile(d)
-        eval_ref[...] = eval_t_ref[...].astype(F32).T.astype(BF16)
 
     def w_copy(d):
         low = d if d <= far else d - far
@@ -218,63 +217,64 @@
             device_id=to_box(d), device_id_type=MESH,
         )
 
-    def local_step(sub, carry):
+    def local_levels(sub, chosen, midway):
         xs, cs, ss = {}, {}, {}
-        for d in order:
+        for d in chosen:
             load_source(sub, d).wait()
-        for d in order:
+        for d in chosen:
             xs[d] = jnp.dot(proj_ref[...], src_ref[sub, d], preferred_element_type=F32)
             cs[d], ss[d] = cos_sin(ang_ref[:, columns(sub, d)].astype(F32)[:n_local])
         for l in range(n_local):
             if l == n_local // 2:
-                @pl.when(sub == 0)
-                def _():
-                    pl.semaphore_wait(barrier, n_box + 1)
-
-                @pl.when(sub == 1)
-                def _():
-                    w_copy(far).wait_recv()
-                    for d in range(far + 1, n_box):
-                        w_copy(d).start()
-
-                @pl.when(sub == n_sub - 1)
-                def _():
-                    q_copy(0).wait_recv()
-                    q_copy(2).start()
-
+                midway()
             matrix = local_w[l]
-            for d in order:
+            for d in chosen:
                 x = xs[d]
                 xs[d] = mix(matrix, x, lane_partner(x, 1 << l), cs[d][l:l + 1], ss[d][l:l + 1])
-        for d in order:
-            snd[sub, d] = xs[d].astype(BF16)
-
-        for d in order:
+        for d in chosen:
             if d:
+                snd[sub, d] = xs[d].astype(BF16)
                 s_copy(sub, d).start()
             else:
                 rcv[sub, me] = xs[0].astype(BF16)
 
-        @pl.when(sub == 0)
-        def _():
-            prepare_aux()
-            for d in range(far, 0, -1):
-                w_copy(d).start()
-            for d in range(n_box - 1, 0, -1):
-                a_copy(d).start()
-
-        @pl.when(sub == 1)
-        def _():
-            for d in range(1, n_box):
-                if d != far:
-                    w_copy(d).wait_recv()
-                a_copy(d).wait_recv()
-            q_copy(0).start()
-            q_copy(1).start()
-
+    def send_aux():
+        pl.semaphore_wait(barrier, n_box + 1)
+        prepare_aux()
+        for d in range(far, 0, -1):
+            w_copy(d).start()
+        for d in range(n_box - 1, 0, -1):
+            a_copy(d).start()
+
+    def forward_aux():
+        w_copy(far).wait_recv()
+        for d in range(far + 1, n_box):
+            w_copy(d).start()
+
+    local_levels(0, order[:far], send_aux)
+    local_levels(0, order[far:], forward_aux)
+
+    def local_step(sub, carry):
+        def share_aux():
+            @pl.when(sub == 1)
+            def _():
+                for d in range(1, n_box):
+                    if d != far:
+                        w_copy(d).wait_recv()
+                    a_copy(d).wait_recv()
+                q_copy(0).start()
+                q_copy(1).start()
+
+            @pl.when(sub == n_sub - 1)
+            def _():
+                q_copy(0).wait_recv()
+                q_copy(2).start()
+
+        local_levels(sub, order, share_aux)
         return carry
 
-    lax.fori_loop(0, n_sub, local_step, 0)
+    lax.fori_loop(1, n_sub, local_step, 0)
+    eval_ref[...] = eval_t_ref[...].astype(F32).T.astype(BF16)
     q_copy(1).wait_recv()
     q_copy(2).wait_recv()
 

time: 37.6 us -> 36.6 us (0.973)
  Pallas kernels: 36.2 us -> 35.1 us
    pallas_call x1, Pallas kernels: 36.2 us -> 35.1 us  [shards(): pl.pallas_call(functools.partial(kernel, n_box), out_shape=pltpu.VMEM((pi...]
where the time goes in v4:
time: 36.6 us; the launch traced here: 36.5 us
  Pallas kernels  35.1 us (96%)
  local copies, waits for them, and re-layouts  1.32 us (4%)
    pallas_call x1, Pallas kernels, shards(): pl.pallas_call(functools.partial(kernel, n_box), out_shape=pltpu.VMEM((pi...  35.1 us
    unnamed x1, local copies, waits for them, and re-layouts  1.32 us

profile of v4, /device:TPU:0, one launch (start us, length us, event | category | flops | bytes accessed | tf_op | source)
XLA Modules:
  0.0 36.5 jit_solution(12080001380594180114)
XLA Ops:
  0.0 35.1 %shard_map.64 = bf16[128,8192]{1,0:T(8,128)(2,1)S(1)} custom-call(bf16[128,8192]{1,0:T(8,128)(2,1)} %src_hbm.1, bf16[64,128]{1,0:T(8,128)(2,1)} %proj_hbm.1, bf16[8,2,64,64]{3,2,1,0:T(8,128)(2,1)} %local_hbm.1, bf16[6,2,64,64]{3,2,1,0:T(8,128)(2,1)} %cross_hbm.1, bf16[14,8192]{1,0:T(8,128)(2,1)} %ang_hbm.1, bf16[64,128]{1,0:T(8,128)(2,1)} %bitcast.1), custom_call_target="tpu_custom_call" | custom-call | flops 2147483648 | bytes 4194304 | tf_op jit(solution)/shard_map/pallas_call | solution.py:331
  35.1 1.3 %copy.8 = bf16[128,8192]{1,0:T(8,128)(2,1)} copy(bf16[128,8192]{1,0:T(8,128)(2,1)S(1)} %shard_map.64) | data formatting | bytes 4194304

commit v5 on v4

--- a/solution.py
+++ b/solution.py
@@ -210,12 +210,16 @@
             device_id=(me, part_y if i == 0 else part_c), device_id_type=MESH,
         )
 
-    def s_copy(sub, d):
+    def s_copy(sub, d, half=None):
+        lanes = pl.ds(0, UNIT) if half is None else pl.ds(half * LANES, LANES)
+        slot = sub if half is None else sub + half
         return pltpu.make_async_remote_copy(
-            src_ref=snd.at[sub, d], dst_ref=rcv.at[sub, me],
-            send_sem=s_snd.at[sub, d], recv_sem=s_rcv.at[sub, d],
+            src_ref=snd.at[sub, d, :, lanes], dst_ref=rcv.at[sub, me, :, lanes],
+            send_sem=s_snd.at[slot, d], recv_sem=s_rcv.at[slot, d],
             device_id=to_box(d), device_id_type=MESH,
         )
+
+    last = n_sub - 1
 
     def local_levels(sub, chosen, midway):
         xs, cs, ss = {}, {}, {}
@@ -234,9 +238,20 @@
         for d in chosen:
             if d:
                 snd[sub, d] = xs[d].astype(BF16)
-                s_copy(sub, d).start()
             else:
                 rcv[sub, me] = xs[0].astype(BF16)
+        away = [d for d in chosen if d]
+
+        @pl.when(sub < last)
+        def _():
+            for d in away:
+                s_copy(sub, d).start()
+
+        @pl.when(sub == last)
+        def _():
+            for half in range(2):
+                for d in away:
+                    s_copy(last, d, half).start()
 
     def send_aux():
         pl.semaphore_wait(barrier, n_box + 1)
@@ -278,14 +293,18 @@
     q_copy(1).wait_recv()
     q_copy(2).wait_recv()
 
-    def cross_step(sub, carry):
-        for d in range(1, n_box):
-            s_copy(sub, d).wait_recv()
-        xs = [rcv[sub, k].astype(F32) for k in range(n_box)]
+    def cross_levels(sub, halves):
+        width = LANES * len(halves)
+        lanes = pl.ds(halves[0] * LANES, width)
+        xs = [rcv[sub, k, :, lanes] for k in range(n_box)]
         tables = [cos_sin(aux[sub, k, w_rows:w_rows + TILE, :].astype(F32)) for k in range(n_box)]
 
-        def row(table, m):
-            return jnp.concatenate([table[m:m + 1], table[8 + m:9 + m]], axis=1)
+        def rows(table, m):
+            row = jnp.concatenate([table[8 * h + m:8 * h + m + 1] for h in halves], axis=1)
+            return jnp.broadcast_to(row, (TILE, width)).astype(BF16)
+
+        def scale(factor, x):
+            return (x.reshape(rank // TILE, TILE, width) * factor[None]).reshape(rank, width)
 
         for m in range(n_cross):
             bit = 1 << (bits - 1 - m) % bits
@@ -295,22 +314,37 @@
                     [aux[q, k, m * TILE:(m + 1) * TILE, :] for q in range(n_sub)], axis=0
                 )
                 cos, sin = tables[k]
-                new.append(mix(matrix, xs[k], xs[k ^ bit], row(cos, m), row(sin, m)))
+                stacked = jnp.concatenate(
+                    [scale(rows(cos, m), xs[k]), scale(rows(sin, m), xs[k ^ bit])], axis=0
+                )
+                new.append(jnp.dot(matrix, stacked, preferred_element_type=F32).astype(BF16))
             xs = new
         for k in range(n_box):
-            pixels = jnp.dot(eval_ref[...], xs[k].astype(BF16), preferred_element_type=F32)
-            start = pl.multiple_of(k * group + sub * UNIT, UNIT)
-            out_ref[:, pl.ds(start, UNIT)] = pixels.astype(BF16)
+            pixels = jnp.dot(eval_ref[...], xs[k], preferred_element_type=F32)
+            start = pl.multiple_of(k * group + sub * UNIT + halves[0] * LANES, LANES)
+            out_ref[:, pl.ds(start, width)] = pixels.astype(BF16)
+
+    def cross_step(sub, carry):
+        for d in range(1, n_box):
+            s_copy(sub, d).wait_recv()
+        cross_levels(sub, (0, 1))
         return carry
 
-    lax.fori_loop(0, n_sub, cross_step, 0)
+    lax.fori_loop(0, last, cross_step, 0)
+    for half in range(2):
+        for d in range(1, n_box):
+            s_copy(last, d, half).wait_recv()
+        cross_levels(last, (half,))
 
     def drain(sub, carry):
         for d in range(1, n_box):
             s_copy(sub, d).wait_send()
         return carry
 
-    lax.fori_loop(0, n_sub, drain, 0)
+    lax.fori_loop(0, last, drain, 0)
+    for half in range(2):
+        for d in range(1, n_box):
+            s_copy(last, d, half).wait_send()
     for d in range(1, n_box):
         w_copy(d).wait_send()
         a_copy(d).wait_send()
@@ -347,7 +381,7 @@
             pltpu.VMEM((n_box, TILE, LANES), BF16),
             pltpu.VMEM((local_mats.shape[0], rank, 2 * rank), BF16),
             dma((5,)), dma((n_sub, n_box)),
-            dma((n_sub, n_box)), dma((n_sub, n_box)),
+            dma((n_sub + 1, n_box)), dma((n_sub + 1, n_box)),
             dma((n_box,)), dma((n_box,)),
             dma((n_box,)), dma((n_box,)),
             dma((3,)), dma((3,)),

time: 36.6 us -> 37.4 us (1.022)
  Pallas kernels: 35.1 us -> 36 us
    pallas_call x1, Pallas kernels: 35.1 us -> 36 us  [shards(): pl.pallas_call(functools.partial(kernel, n_box), out_shape=pltpu.VMEM((pi...]
where the time goes in v5:
time: 37.4 us; the launch traced here: 37.3 us
  Pallas kernels  36 us (96%)
  local copies, waits for them, and re-layouts  1.32 us (4%)
    pallas_call x1, Pallas kernels, shards(): pl.pallas_call(functools.partial(kernel, n_box), out_shape=pltpu.VMEM((pi...  36 us
    unnamed x1, local copies, waits for them, and re-layouts  1.32 us

profile of v5, /device:TPU:0, one launch (start us, length us, event | category | flops | bytes accessed | tf_op | source)
XLA Modules:
  0.0 37.3 jit_solution(17568860731999590472)
XLA Ops:
  0.0 36.0 %shard_map.64 = bf16[128,8192]{1,0:T(8,128)(2,1)S(1)} custom-call(bf16[128,8192]{1,0:T(8,128)(2,1)} %src_hbm.1, bf16[64,128]{1,0:T(8,128)(2,1)} %proj_hbm.1, bf16[8,2,64,64]{3,2,1,0:T(8,128)(2,1)} %local_hbm.1, bf16[6,2,64,64]{3,2,1,0:T(8,128)(2,1)} %cross_hbm.1, bf16[14,8192]{1,0:T(8,128)(2,1)} %ang_hbm.1, bf16[64,128]{1,0:T(8,128)(2,1)} %bitcast.1), custom_call_target="tpu_custom_call" | custom-call | flops 2147483648 | bytes 4194304 | tf_op jit(solution)/shard_map/pallas_call | solution.py:365
  36.0 1.3 %copy.8 = bf16[128,8192]{1,0:T(8,128)(2,1)} copy(bf16[128,8192]{1,0:T(8,128)(2,1)S(1)} %shard_map.64) | data formatting | bytes 4194304

commit v6 on v4

--- a/solution.py
+++ b/solution.py
@@ -217,6 +217,25 @@
             device_id=to_box(d), device_id_type=MESH,
         )
 
+    def send(sub, chosen):
+        away = [d for d in chosen if d]
+        far_ones = [d for d in away if d >= far]
+        near_ones = [d for d in away if d < far]
+        core = lax.rem(part, 2)
+
+        def start(first, second):
+            for i in range(max(len(first), len(second))):
+                for d in first[i:i + 1] + second[i:i + 1]:
+                    s_copy(sub, d).start()
+
+        @pl.when(core == 0)
+        def _():
+            start(far_ones, near_ones)
+
+        @pl.when(core == 1)
+        def _():
+            start(near_ones, far_ones)
+
     def local_levels(sub, chosen, midway):
         xs, cs, ss = {}, {}, {}
         for d in chosen:
@@ -234,9 +253,9 @@
         for d in chosen:
             if d:
                 snd[sub, d] = xs[d].astype(BF16)
-                s_copy(sub, d).start()
             else:
                 rcv[sub, me] = xs[0].astype(BF16)
+        send(sub, chosen)
 
     def send_aux():
         pl.semaphore_wait(barrier, n_box + 1)
@@ -278,32 +297,47 @@
     q_copy(1).wait_recv()
     q_copy(2).wait_recv()
 
-    def cross_step(sub, carry):
-        for d in range(1, n_box):
-            s_copy(sub, d).wait_recv()
-        xs = [rcv[sub, k].astype(F32) for k in range(n_box)]
-        tables = [cos_sin(aux[sub, k, w_rows:w_rows + TILE, :].astype(F32)) for k in range(n_box)]
-
-        def row(table, m):
-            return jnp.concatenate([table[m:m + 1], table[8 + m:9 + m]], axis=1)
-
+    def rows(table, m):
+        row = jnp.concatenate([table[m:m + 1], table[8 + m:9 + m]], axis=1)
+        return jnp.broadcast_to(row, (TILE, UNIT)).astype(BF16)
+
+    def scale(factor, x):
+        return (x.reshape(rank // TILE, TILE, UNIT) * factor[None]).reshape(rank, UNIT)
+
+    def cross_levels(subs):
+        for sub in subs:
+            for d in range(1, n_box):
+                s_copy(sub, d).wait_recv()
+        chains = [(sub, k) for sub in subs for k in range(n_box)]
+        xs = {c: rcv[c[0], c[1]] for c in chains}
+        tables = {
+            (sub, k): cos_sin(aux[sub, k, w_rows:w_rows + TILE, :].astype(F32)) for sub, k in chains
+        }
         for m in range(n_cross):
             bit = 1 << (bits - 1 - m) % bits
-            new = []
+            new = {}
             for k in range(n_box):
                 matrix = jnp.concatenate(
                     [aux[q, k, m * TILE:(m + 1) * TILE, :] for q in range(n_sub)], axis=0
                 )
-                cos, sin = tables[k]
-                new.append(mix(matrix, xs[k], xs[k ^ bit], row(cos, m), row(sin, m)))
+                for sub in subs:
+                    cos, sin = tables[sub, k]
+                    stacked = jnp.concatenate(
+                        [
+                            scale(rows(cos, m), xs[sub, k]),
+                            scale(rows(sin, m), xs[sub, k ^ bit]),
+                        ],
+                        axis=0,
+                    )
+                    mixed = jnp.dot(matrix, stacked, preferred_element_type=F32)
+                    new[sub, k] = mixed.astype(BF16)
             xs = new
-        for k in range(n_box):
-            pixels = jnp.dot(eval_ref[...], xs[k].astype(BF16), preferred_element_type=F32)
-            start = pl.multiple_of(k * group + sub * UNIT, UNIT)
-            out_ref[:, pl.ds(start, UNIT)] = pixels.astype(BF16)
-        return carry
-
-    lax.fori_loop(0, n_sub, cross_step, 0)
+        for sub, k in chains:
+            pixels = jnp.dot(eval_ref[...], xs[sub, k], preferred_element_type=F32)
+            out_ref[:, k * group + sub * UNIT:k * group + (sub + 1) * UNIT] = pixels.astype(BF16)
+
+    for subs in [(0, 1)] + [(sub,) for sub in range(2, n_sub)]:
+        cross_levels(subs)
 
     def drain(sub, carry):
         for d in range(1, n_box):

time: 36.6 us -> 37 us (1.011)
  Pallas kernels: 35.1 us -> 35.5 us
    pallas_call x1, Pallas kernels: 35.1 us -> 35.5 us  [shards(): pl.pallas_call(functools.partial(kernel, n_box), out_shape=pltpu.VMEM((pi...]
where the time goes in v6:
time: 37 us; the launch traced here: 36.8 us
  Pallas kernels  35.5 us (96%)
  local copies, waits for them, and re-layouts  1.32 us (4%)
    pallas_call x1, Pallas kernels, shards(): pl.pallas_call(functools.partial(kernel, n_box), out_shape=pltpu.VMEM((pi...  35.5 us
    unnamed x1, local copies, waits for them, and re-layouts  1.32 us

profile of v6, /device:TPU:0, one launch (start us, length us, event | category | flops | bytes accessed | tf_op | source)
XLA Modules:
  0.0 36.8 jit_solution(8773314769172380456)
XLA Ops:
  0.0 35.5 %shard_map.64 = bf16[128,8192]{1,0:T(8,128)(2,1)S(1)} custom-call(bf16[128,8192]{1,0:T(8,128)(2,1)} %src_hbm.1, bf16[64,128]{1,0:T(8,128)(2,1)} %proj_hbm.1, bf16[8,2,64,64]{3,2,1,0:T(8,128)(2,1)} %local_hbm.1, bf16[6,2,64,64]{3,2,1,0:T(8,128)(2,1)} %cross_hbm.1, bf16[14,8192]{1,0:T(8,128)(2,1)} %ang_hbm.1, bf16[64,128]{1,0:T(8,128)(2,1)} %bitcast.1), custom_call_target="tpu_custom_call" | custom-call | flops 2147483648 | bytes 4194304 | tf_op jit(solution)/shard_map/pallas_call | solution.py:365
  35.5 1.3 %copy.8 = bf16[128,8192]{1,0:T(8,128)(2,1)} copy(bf16[128,8192]{1,0:T(8,128)(2,1)S(1)} %shard_map.64) | data formatting | bytes 4194304

commit v7 on v4

--- a/solution.py
+++ b/solution.py
@@ -217,21 +217,21 @@
             device_id=to_box(d), device_id_type=MESH,
         )
 
-    def local_levels(sub, chosen, midway):
+    def local_levels(chosen, midway):
         xs, cs, ss = {}, {}, {}
-        for d in chosen:
+        for sub, d in chosen:
             load_source(sub, d).wait()
-        for d in chosen:
+        for sub, d in chosen:
             xs[d] = jnp.dot(proj_ref[...], src_ref[sub, d], preferred_element_type=F32)
             cs[d], ss[d] = cos_sin(ang_ref[:, columns(sub, d)].astype(F32)[:n_local])
         for l in range(n_local):
             if l == n_local // 2:
                 midway()
             matrix = local_w[l]
-            for d in chosen:
+            for _, d in chosen:
                 x = xs[d]
                 xs[d] = mix(matrix, x, lane_partner(x, 1 << l), cs[d][l:l + 1], ss[d][l:l + 1])
-        for d in chosen:
+        for sub, d in chosen:
             if d:
                 snd[sub, d] = xs[d].astype(BF16)
                 s_copy(sub, d).start()
@@ -251,12 +251,21 @@
         for d in range(far + 1, n_box):
             w_copy(d).start()
 
-    local_levels(0, order[:far], send_aux)
-    local_levels(0, order[far:], forward_aux)
+    def far_units(sub):
+        return [(sub, d) for d in order[:far]]
+
+    def near_units(sub):
+        return [(sub, d) for d in order[far:]]
+
+    local_levels(far_units(0), send_aux)
 
     def local_step(sub, carry):
-        def share_aux():
+        def move_aux():
             @pl.when(sub == 1)
+            def _():
+                forward_aux()
+
+            @pl.when(sub == 2)
             def _():
                 for d in range(1, n_box):
                     if d != far:
@@ -265,15 +274,15 @@
                 q_copy(0).start()
                 q_copy(1).start()
 
-            @pl.when(sub == n_sub - 1)
-            def _():
-                q_copy(0).wait_recv()
-                q_copy(2).start()
-
-        local_levels(sub, order, share_aux)
+        local_levels(far_units(sub) + near_units(sub - 1), move_aux)
         return carry
 
+    def finish_aux():
+        q_copy(0).wait_recv()
+        q_copy(2).start()
+
     lax.fori_loop(1, n_sub, local_step, 0)
+    local_levels(near_units(n_sub - 1), finish_aux)
     eval_ref[...] = eval_t_ref[...].astype(F32).T.astype(BF16)
     q_copy(1).wait_recv()
     q_copy(2).wait_recv()

time: 36.6 us -> 36 us (0.984)
  Pallas kernels: 35.1 us -> 34.6 us
    pallas_call x1, Pallas kernels: 35.1 us -> 34.6 us  [shards(): pl.pallas_call(functools.partial(kernel, n_box), out_shape=pltpu.VMEM((pi...]
where the time goes in v7:
time: 36 us; the launch traced here: 35.9 us
  Pallas kernels  34.6 us (96%)
  local copies, waits for them, and re-layouts  1.32 us (4%)
    pallas_call x1, Pallas kernels, shards(): pl.pallas_call(functools.partial(kernel, n_box), out_shape=pltpu.VMEM((pi...  34.6 us
    unnamed x1, local copies, waits for them, and re-layouts  1.32 us

profile of v7, /device:TPU:0, one launch (start us, length us, event | category | flops | bytes accessed | tf_op | source)
XLA Modules:
  0.0 35.9 jit_solution(14091215663621567565)
XLA Ops:
  0.0 34.6 %shard_map.64 = bf16[128,8192]{1,0:T(8,128)(2,1)S(1)} custom-call(bf16[128,8192]{1,0:T(8,128)(2,1)} %src_hbm.1, bf16[64,128]{1,0:T(8,128)(2,1)} %proj_hbm.1, bf16[8,2,64,64]{3,2,1,0:T(8,128)(2,1)} %local_hbm.1, bf16[6,2,64,64]{3,2,1,0:T(8,128)(2,1)} %cross_hbm.1, bf16[14,8192]{1,0:T(8,128)(2,1)} %ang_hbm.1, bf16[64,128]{1,0:T(8,128)(2,1)} %bitcast.1), custom_call_target="tpu_custom_call" | custom-call | flops 2147483648 | bytes 4194304 | tf_op jit(solution)/shard_map/pallas_call | solution.py:340
  34.6 1.3 %copy.8 = bf16[128,8192]{1,0:T(8,128)(2,1)} copy(bf16[128,8192]{1,0:T(8,128)(2,1)S(1)} %shard_map.64) | data formatting | bytes 4194304

commit v8 on v7

--- a/solution.py
+++ b/solution.py
@@ -217,7 +217,7 @@
             device_id=to_box(d), device_id_type=MESH,
         )
 
-    def local_levels(chosen, midway):
+    def local_levels(chosen, midway, at=n_local // 2):
         xs, cs, ss = {}, {}, {}
         for sub, d in chosen:
             load_source(sub, d).wait()
@@ -225,7 +225,7 @@
             xs[d] = jnp.dot(proj_ref[...], src_ref[sub, d], preferred_element_type=F32)
             cs[d], ss[d] = cos_sin(ang_ref[:, columns(sub, d)].astype(F32)[:n_local])
         for l in range(n_local):
-            if l == n_local // 2:
+            if l == at:
                 midway()
             matrix = local_w[l]
             for _, d in chosen:
@@ -257,7 +257,7 @@
     def near_units(sub):
         return [(sub, d) for d in order[far:]]
 
-    local_levels(far_units(0), send_aux)
+    local_levels(far_units(0), send_aux, n_local // 4)
 
     def local_step(sub, carry):
         def move_aux():

time: 36 us -> 35.4 us (0.983)
  Pallas kernels: 34.6 us -> 33.9 us
    pallas_call x1, Pallas kernels: 34.6 us -> 33.9 us  [shards(): pl.pallas_call(functools.partial(kernel, n_box), out_shape=pltpu.VMEM((pi...]
where the time goes in v8:
time: 35.4 us; the launch traced here: 35.3 us
  Pallas kernels  33.9 us (96%)
  local copies, waits for them, and re-layouts  1.32 us (4%)
    pallas_call x1, Pallas kernels, shards(): pl.pallas_call(functools.partial(kernel, n_box), out_shape=pltpu.VMEM((pi...  33.9 us
    unnamed x1, local copies, waits for them, and re-layouts  1.32 us

profile of v8, /device:TPU:0, one launch (start us, length us, event | category | flops | bytes accessed | tf_op | source)
XLA Modules:
  0.0 35.3 jit_solution(11952735750257194129)
XLA Ops:
  0.0 33.9 %shard_map.64 = bf16[128,8192]{1,0:T(8,128)(2,1)S(1)} custom-call(bf16[128,8192]{1,0:T(8,128)(2,1)} %src_hbm.1, bf16[64,128]{1,0:T(8,128)(2,1)} %proj_hbm.1, bf16[8,2,64,64]{3,2,1,0:T(8,128)(2,1)} %local_hbm.1, bf16[6,2,64,64]{3,2,1,0:T(8,128)(2,1)} %cross_hbm.1, bf16[14,8192]{1,0:T(8,128)(2,1)} %ang_hbm.1, bf16[64,128]{1,0:T(8,128)(2,1)} %bitcast.1), custom_call_target="tpu_custom_call" | custom-call | flops 2147483648 | bytes 4194304 | tf_op jit(solution)/shard_map/pallas_call | solution.py:340
  33.9 1.3 %copy.8 = bf16[128,8192]{1,0:T(8,128)(2,1)} copy(bf16[128,8192]{1,0:T(8,128)(2,1)S(1)} %shard_map.64) | data formatting | bytes 4194304
